TPU v7x, 32 devices: a whole 2x2x4 slice. The times are simulated.
32 devices in a mesh: section: 16 (over z, x, core), team: 2 (over y).
Axes of the slice: x: 2, y: 2, z: 4, core: 2. Of those that a mesh axis runs over, the one named last changes fastest.
Arguments:
- amps: bfloat16 [1024, 8192], P('team', 'section'), may hold values from -6 to 6
- t_mask: int32 [8, 64], P('team', 'section'), may hold values from 0 to 1, as said below
- ints: bfloat16 [8192, 8192], P('team', 'section'), may hold values from -0.09375 to 0.09375
- v_mask: int32 [64, 64], P('team', 'section'), may hold values 0 or 1
Outputs:
- ladder: bfloat16 [1024, 8192], P('team', 'section')
Inputs may be any that keep to these rules, and one draw needn't show every extreme that they name: `t_mask`: in every row of tiles, each aligned group of 4 tile columns holds exactly 2 ones; which ones is random.
All inputs are finite; a program needn't handle non-finite values. No bound on the sum of `v_mask` on one device may be relied on, other than what follows from the above.
Results may differ from a plain program's by a relative error of at most 0.001.
Values may be sent and summed in bfloat16 or wider, within the bound.
A program may use at most 128 MiB of HBM per device.

v0:
```python
import jax
import jax.numpy as jnp
from jax import lax
from jax.sharding import PartitionSpec as P

TILE = 128
NZ = 2


def expand_mask(values, mask):
    rows, cols = values.shape
    tiles = values.reshape(rows // TILE, TILE, cols // TILE, TILE)
    scaled = tiles * mask.astype(values.dtype)[:, None, :, None]
    return scaled.reshape(rows, cols)


def slot_table(mask):
    position = jnp.cumsum(mask, axis=-1) - 1
    slots = jnp.arange(NZ, dtype=jnp.int32)
    hit = (mask[..., None, :] == 1) & (position[..., None, :] == slots[:, None])
    return hit.astype(jnp.bfloat16)


def shards(amps, t_mask, ints, v_mask):
    occ_rows, panel = amps.shape
    ab_cols = ints.shape[1]
    row_tiles = occ_rows // TILE
    panel_tiles = panel // TILE
    int_full, mask_full = (
        lax.all_gather(ints, "team", axis=0, tiled=True),
        lax.all_gather(v_mask, "team", axis=0, tiled=True),
    )
    v_eff = expand_mask(int_full, mask_full)
    total_rows = v_eff.shape[0]
    v_tiles = v_eff.reshape(total_rows // panel, panel_tiles, TILE, ab_cols)
    local_mask = t_mask.reshape(row_tiles, 1, panel_tiles)
    select = slot_table(t_mask)
    tiles = amps.reshape(row_tiles, TILE, panel_tiles, TILE)
    packed = jnp.einsum("rjc,rxcy->rxjy", select, tiles, preferred_element_type=jnp.float32).astype(
        jnp.bfloat16
    )
    packed = packed.reshape(occ_rows, 1, NZ * TILE)
    values = lax.all_gather(packed, "section", axis=1, tiled=True)
    masks = lax.all_gather(local_mask, "section", axis=1, tiled=True)
    count = values.shape[1]
    picks = slot_table(masks)
    chosen = jnp.einsum(
        "rkjc,kcya->rkjya", picks, v_tiles, preferred_element_type=jnp.float32
    ).astype(jnp.bfloat16)
    shaped = values.reshape(row_tiles, TILE, count, NZ, TILE)
    term = jnp.einsum("rxkjy,rkjya->rxa", shaped, chosen, preferred_element_type=jnp.float32)
    total = term.reshape(occ_rows, ab_cols)
    return total.astype(jnp.bfloat16)


def solution(mesh):
    in_specs = (
        P("team", "section"),
        P("team", "section"),
        P("team", "section"),
        P("team", "section"),
    )
    out_specs = P("team", "section")
    return jax.shard_map(shards, mesh=mesh, in_specs=in_specs, out_specs=out_specs, check_vma=False)
```

profile of v0, /device:TPU:0, one launch (start us, length us, event | category | flops | bytes accessed | tf_op | source)
XLA Modules:
  0.0 212.4 jit_solution(364956112359081148)
XLA Ops:
  6.5 0.0 all-gather.6.cloned.1.call-start
  6.5 1.2 reshape.36
  7.7 0.7 broadcast_compare_fusion.1
  8.4 0.9 reduce_window_sum.24
  9.3 0.4 fusion.16
  9.7 0.9 reshape.37
  10.6 0.0 all-gather.6.cloned.1.call-update
  10.6 0.0 all-gather.8.cloned.1.call-start
  10.6 0.7 all-gather.8.cloned.1.call-update
  11.3 0.8 copy.37
  12.1 23.4 %all-gather.2 = s32[16,4,4]{2,1,0:T(4,128)S(1)} all-gather(s32[1,4,4]{2,1,0:T(4,128)S(1)} %bitcast.48), channel_id=2, replica_groups=mesh['section'=16,'team'=2] {'section'}, dimensions={0}, use_global_device_ids=true | all-gather | bytes 1088 | tf_op jit(solution)/shard_map/all_gather | solution.py:44
  35.5 0.1 copy.38
  35.6 0.1 reshape.40
  35.7 0.7 reduce_window_sum.26
  36.4 4.5 %all-gather.1 = s32[2,32,4]{1,2,0:T(4,128)S(1)} all-gather(s32[1,32,4]{1,2,0:T(4,128)} %bitcast.49), channel_id=1, replica_groups=mesh['section'=16,'team'=2] {'team'}, dimensions={0}, use_global_device_ids=true | all-gather | bytes 1536 | tf_op jit(solution)/shard_map/all_gather | solution.py:31
  40.9 0.1 copy.50
  41.0 0.1 mul.13
  41.2 22.9 %all-gather.6.cloned.1.call-done = bf16[512,16,256]{2,0,1:T(8,128)(2,1)} async-done(((bf16[512,1,256]{2,0,1:T(8,128)(2,1)}), bf16[512,16,256]{2,0,1:T(8,128)(2,1)}) %all-gather.6.cloned.1.call-update) | async-done | bytes 4194320 | tf_op jit(solution)/shard_map/all_gather | solution.py:43
  64.1 7.0 %reshape.50 = bf16[4,128,16,2,128]{4,3,1,0,2:T(2,128)(2,1)} reshape(bf16[512,16,256]{2,0,1:T(8,128)(2,1)} %all-gather.6.cloned.1.call-done) | data formatting | bytes 8388608 | tf_op jit(solution)/shard_map/reshape | solution.py:50
  71.1 97.1 %all-gather.8.cloned.1.call-done = bf16[8192,512]{1,0:T(8,128)(2,1)} async-done(((bf16[4096,512]{1,0:T(8,128)(2,1)}), bf16[8192,512]{1,0:T(8,128)(2,1)}) %all-gather.8.cloned.1.call-update) | async-done | bytes 8388624 | tf_op jit(solution)/shard_map/all_gather | solution.py:30
  168.2 0.0 copy-start
  168.2 21.3 %fusion = bf16[4,16,2,128,512]{4,2,0,3,1:T(2,128)(2,1)} fusion(bf16[16,4,128,512]{3,2,1,0:T(8,128)(2,1)} %bitcast.50, bf16[16,4,512]{2,1,0:T(4,128)(2,1)S(1)} %mul.14, pred[4,16,4]{2,0,1:T(4,128)(4,1)S(1)} %copy.40, s32[4,16,4]{2,0,1:T(4,128)S(1)} %copy.41), kind=kOutput, calls=%fused_computation.1 | convolution fusion | flops 92275712 | bytes 25232640 | tf_op jit(solution)/shard_map/rkjc,kcya->rkjya/dot_general | solution.py:47
  189.5 0.0 copy-done
  189.5 16.0 %fusion.11 = bf16[4,128,512]{2,1,0:T(8,128)(2,1)} fusion(bf16[4,16,2,128,512]{4,2,0,3,1:T(2,128)(2,1)} %fusion, bf16[4,128,16,2,128]{4,3,1,0,2:T(2,128)(2,1)S(1)} %copy-done), kind=kOutput, calls=%fused_computation.9 | convolution fusion | flops 2147745792 | bytes 21495808 | tf_op jit(solution)/shard_map/rxkjy,rkjya->rxa/dot_general | solution.py:51
  (7 shorter events, 0.1 us)
Async XLA Ops:
  6.5 57.5 %all-gather.6.cloned.1.call-start = ((), (), s32[]{:S(2)}) async-start(), calls=%async_computation | async-start | bytes 4456448 | tf_op jit(solution)/shard_map/all_gather | solution.py:43
  10.6 157.6 %all-gather.8.cloned.1.call-start = ((), (), s32[]{:S(2)}) async-start(), calls=%async_computation.1 | async-start | bytes 12582912 | tf_op jit(solution)/shard_map/all_gather | solution.py:30
  168.2 21.3 %copy-start = (bf16[4,128,16,2,128]{4,3,1,0,2:T(2,128)(2,1)S(1)}, bf16[4,128,16,2,128]{4,3,1,0,2:T(2,128)(2,1)}, u32[]{:S(2)}) copy-start(bf16[4,128,16,2,128]{4,3,1,0,2:T(2,128)(2,1)} %reshape.50) | copy-start | bytes 12582916
Sparse Core Ops, SparseCore 0:
  10.7 53.3 all-gather.5
  65.6 102.4 all-gather.7
where the time goes:
time: 213 us; the launch traced here: 212 us
  waiting for transfers between devices  121 us (57%)
  matrix products  37.8 us (18%)
  blocking collectives  27.9 us (13%)
  between operations  13.5 us (6%)
  local copies, waits for them, and re-layouts  10.3 us (5%)
  other arithmetic  2.22 us (1%)
    all_gather x1, waiting for transfers between devices, shards(): lax.all_gather(ints, 'team', axis=0, tiled=True)  97.1 us
    all_gather x1, blocking collectives, shards(): masks = lax.all_gather(local_mask, 'section', axis=1, tiled=True)  23.4 us
    all_gather x1, waiting for transfers between devices, shards(): values = lax.all_gather(packed, 'section', axis=1, tiled=True)  22.9 us
    dot_general x1, matrix products, shards(): jnp.einsum('rkjc,kcya->rkjya', picks, v_tiles, preferred_element_type=jnp...  21.3 us
    dot_general x1, matrix products, shards(): jnp.einsum('rxkjy,rkjya->rxa', shaped, chosen, preferred_element_type=jnp...  16 us
    reshape x1, local copies, waits for them, and re-layouts, shards(): shaped = values.reshape(row_tiles, TILE, count, NZ, TILE)  7 us
    all_gather x1, blocking collectives, shards(): lax.all_gather(v_mask, 'team', axis=0, tiled=True)  4.47 us
  transfers between devices with their start and end apart: 2, of which 2 were waited for; matrix products, arithmetic and copies ran while one was open for 4% of the time, Pallas kernels for 0%

commit v1 on v0

v1 whole, which is shorter than its diff:
```python
import functools

import jax
import jax.numpy as jnp
from jax import lax
from jax.experimental import pallas as pl
from jax.experimental.pallas import tpu as pltpu
from jax.sharding import PartitionSpec as P

TILE = 128
NZ = 2
CORES = 2
MESH = pl.DeviceIdType.MESH


def kernel(sections, teams, columns, amps_ref, tm_ref, vm_ref, ints_ref, out_ref,
           mine, buf, v, texp, acc, part, got, load_sem, y_sem, send_sem, recv_sem, part_sem, got_sem):
    rows, panel = amps_ref.shape
    row_tiles, tiles = rows // TILE, panel // TILE
    share = sections // teams
    levels = sections // (CORES * columns)
    s, t = lax.axis_index("section"), lax.axis_index("team")
    core, chip = lax.rem(s, CORES), lax.div(s, CORES)
    x, z = lax.rem(chip, columns), lax.div(chip, columns)
    group = lax.div(s, share)
    sibling = s + 1 - 2 * core

    def at(section, team):
        return {"section": section, "team": team}

    load = pltpu.make_async_copy(ints_ref, v, load_sem)
    load.start()

    barrier = pltpu.get_barrier_semaphore()

    def greet(section, team):
        pl.semaphore_signal(barrier, inc=1, device_id=at(section, team), device_id_type=MESH)

    greet(sibling, t)
    for d in range(1, columns):
        greet(s + CORES * (lax.rem(x + d, columns) - x), t)
    for d in range(1, teams):
        greet(s, lax.rem(t + d, teams))
    step = CORES * columns

    @pl.when(z > 0)
    def _():
        greet(s - step, t)

    @pl.when(z < levels - 1)
    def _():
        greet(s + step, t)

    partners = 1 + (columns - 1) + (teams - 1)
    partners = partners + jnp.where(z > 0, 1, 0) + jnp.where(z < levels - 1, 1, 0)

    shape = (row_tiles * tiles, NZ * TILE)
    table_row = lax.broadcasted_iota(jnp.int32, shape, 0)
    table_lane = lax.broadcasted_iota(jnp.int32, shape, 1)
    hits = jnp.zeros(shape, jnp.float32)
    for i in range(row_tiles):
        before = jnp.int32(0)
        for c in range(tiles):
            one = tm_ref[i, c]
            for j in range(NZ):
                hit = jnp.where(before == j, one, 0).astype(jnp.float32)
                place = (table_row == i * tiles + c) & (table_lane >= j * TILE) & (table_lane < (j + 1) * TILE)
                hits = jnp.where(place, hit, hits)
            before = before + one

    def spread(table, i, c, j):
        row = table[i * tiles + c : i * tiles + c + 1, j * TILE : (j + 1) * TILE]
        return jnp.broadcast_to(row.astype(jnp.bfloat16), (TILE, TILE))

    for i in range(row_tiles):
        for j in range(NZ):
            total = None
            for c in range(tiles):
                tile = amps_ref[i * TILE : (i + 1) * TILE, c * TILE : (c + 1) * TILE]
                term = tile * spread(hits, i, c, j)
                total = term if total is None else total + term
            mine[i * TILE : (i + 1) * TILE, j * TILE : (j + 1) * TILE] = total
    mine[rows:, :] = hits.astype(jnp.bfloat16)
    own = t * share + lax.rem(s, share)

    @pl.when(group == t)
    def _():
        buf[own] = mine[...]

    pl.semaphore_wait(barrier, partners)

    def y_copy():
        return pltpu.make_async_remote_copy(
            src_ref=mine, dst_ref=buf.at[own], send_sem=y_sem, recv_sem=recv_sem.at[own],
            device_id=at(s, group), device_id_type=MESH)

    @pl.when(group != t)
    def _():
        y_copy().start()

    def slot(n):
        i, u = lax.div(n, share), lax.rem(n, share)
        source = lax.rem(t + 1 + i, teams)
        return source, u, source * share + u, t * share + u

    def forward(n, go):
        source, u, k, home = slot(n)
        home_core, home_chip = lax.rem(home, CORES), lax.div(home, CORES)
        home_x, home_z = lax.rem(home_chip, columns), lax.div(home_chip, columns)
        straight = core == home_core
        column = straight & (x == home_x)

        def copy(kind, section):
            return pltpu.make_async_remote_copy(
                src_ref=buf.at[k], dst_ref=buf.at[k], send_sem=send_sem.at[kind, k], recv_sem=recv_sem.at[k],
                device_id=at(section, t), device_id_type=MESH)

        @pl.when(column & (z >= home_z) & (z < levels - 1))
        def _():
            go(copy(0, s + step))

        @pl.when(column & (z <= home_z) & (z > 0))
        def _():
            go(copy(1, s - step))

        for d in range(1, columns):
            @pl.when(column)
            def _():
                go(copy(2 + d, s + CORES * (lax.rem(x + d, columns) - x)))

        @pl.when(straight)
        def _():
            go(copy(2, sibling))

    def arrive(n):
        source, u, k, home = slot(n)

        @pl.when((s != home) | (source != t))
        def _():
            pltpu.make_async_remote_copy(
                src_ref=buf.at[k], dst_ref=buf.at[k], send_sem=send_sem.at[2, k], recv_sem=recv_sem.at[k],
                device_id=at(sibling, t), device_id_type=MESH).wait_recv()

    load.wait()

    @pl.loop(0, v.shape[0] // TILE)
    def _(k):
        here = pl.ds(pl.multiple_of(k * TILE, TILE), TILE)
        for c in range(v.shape[1] // TILE):
            lanes = slice(c * TILE, (c + 1) * TILE)
            v[here, lanes] = v[here, lanes] * jnp.full((TILE, TILE), vm_ref[k, c].astype(jnp.float32)).astype(jnp.bfloat16)

    def part_copy(d):
        return pltpu.make_async_remote_copy(
            src_ref=part.at[d - 1], dst_ref=got.at[teams - d - 1], send_sem=part_sem.at[d - 1],
            recv_sem=got_sem.at[teams - d - 1], device_id=at(s, lax.rem(t + d, teams)), device_id_type=MESH)

    def one_team(d):
        acc[...] = jnp.zeros_like(acc)

        @pl.loop(0, share)
        def _(u):
            n = (d - 1) * share + u
            arrive(n)
            forward(n, lambda copy: copy.start())
            _, _, k, _ = slot(n)
            table = buf[k, rows:, :].astype(jnp.float32)
            for i in range(row_tiles):
                for c in range(tiles):
                    tile = None
                    for j in range(NZ):
                        term = buf[k, i * TILE : (i + 1) * TILE, j * TILE : (j + 1) * TILE] * spread(table, i, c, j)
                        tile = term if tile is None else tile + term
                    texp[i * TILE : (i + 1) * TILE, c * TILE : (c + 1) * TILE] = tile
            here = pl.ds(pl.multiple_of(u * panel, panel), panel)
            acc[...] += jnp.dot(texp[...], v[here, :], preferred_element_type=jnp.float32)

    for d in range(1, teams):
        one_team(d)
        part[d - 1] = acc[...]
        part_copy(d).start()
    one_team(teams)
    for d in range(1, teams):
        part_copy(d).wait_recv()
        acc[...] += got[teams - d - 1]
    out_ref[...] = acc[...].astype(out_ref.dtype)

    @pl.when(group != t)
    def _():
        y_copy().wait_send()

    @pl.loop(0, teams * share)
    def _(n):
        forward(n, lambda copy: copy.wait_send())

    for d in range(1, teams):
        part_copy(d).wait_send()


def shards(sections, teams, columns, amps, t_mask, ints, v_mask):
    rows, panel = amps.shape
    depth, ab_cols = ints.shape
    slots = sections
    message = (rows + t_mask.shape[0] * t_mask.shape[1], NZ * TILE)
    smem = pl.BlockSpec(memory_space=pltpu.SMEM)
    vmem = pl.BlockSpec(memory_space=pltpu.VMEM)
    return pl.pallas_call(
        functools.partial(kernel, sections, teams, columns),
        out_shape=jax.ShapeDtypeStruct((rows, ab_cols), jnp.bfloat16),
        in_specs=[vmem, smem, smem, pl.BlockSpec(memory_space=pl.ANY)],
        out_specs=vmem,
        scratch_shapes=[
            pltpu.VMEM(message, jnp.bfloat16),
            pltpu.VMEM((slots, *message), jnp.bfloat16),
            pltpu.VMEM((depth, ab_cols), jnp.bfloat16),
            pltpu.VMEM((rows, panel), jnp.bfloat16),
            pltpu.VMEM((rows, ab_cols), jnp.float32),
            pltpu.VMEM((teams - 1, rows, ab_cols), jnp.float32),
            pltpu.VMEM((teams - 1, rows, ab_cols), jnp.float32),
            pltpu.SemaphoreType.DMA,
            pltpu.SemaphoreType.DMA,
            pltpu.SemaphoreType.DMA((2 + columns, slots)),
            pltpu.SemaphoreType.DMA((slots,)),
            pltpu.SemaphoreType.DMA((teams - 1,)),
            pltpu.SemaphoreType.DMA((teams - 1,)),
        ],
        compiler_params=pltpu.CompilerParams(
            collective_id=0, has_side_effects=True, vmem_limit_bytes=48 * 2**20
        ),
        cost_estimate=pl.CostEstimate(
            flops=2 * teams * rows * depth * ab_cols, bytes_accessed=2 * depth * ab_cols, transcendentals=0
        ),
    )(amps, t_mask, v_mask, ints)


def solution(mesh):
    sections, teams = mesh.shape["section"], mesh.shape["team"]
    chips = sections // CORES
    columns = 1
    while (2 * columns) ** 2 <= chips and chips % (2 * columns) == 0:
        columns *= 2
    spec = P("team", "section")
    return jax.shard_map(
        functools.partial(shards, sections, teams, columns),
        mesh=mesh, in_specs=(spec,) * 4, out_specs=spec, check_vma=False)
```

time: 213 us -> 143 us (0.67)
  the two profiles are of different devices: /device:TPU:0 before, /device:TPU:4 now
where the time goes in v1:
time: 143 us
  Pallas kernels  138 us (97%)
  local copies, waits for them, and re-layouts  5.47 us (4%)
    pallas_call x1, Pallas kernels, shards(): pl.pallas_call(functools.partial(kernel, sections, teams, columns), out_s...  138 us
    unnamed x8, local copies, waits for them, and re-layouts  5.47 us

profile of v1, /device:TPU:4, one launch (start us, length us, event | category | flops | bytes accessed | tf_op | source)
XLA Modules:
  0.0 143.2 jit_solution(15977250243159849893)
XLA Ops:
  0.0 0.8 copy.5.vm_ref
  0.8 0.0 copy-start
  0.8 2.2 %copy-done = bf16[4096,512]{1,0:T(8,128)(2,1)S(1)} copy-done((bf16[4096,512]{1,0:T(8,128)(2,1)S(1)}, bf16[4096,512]{1,0:T(8,128)(2,1)}, u32[]{:S(2)}) %copy-start) | copy-done | bytes 4194328
  3.0 0.0 copy-start.1
  3.0 1.0 copy-done.1
  4.0 0.0 copy-start.2
  4.0 0.7 copy-done.2
  4.7 137.7 %shard_map.46 = bf16[512,512]{1,0:T(8,128)(2,1)S(1)} custom-call(bf16[512,512]{1,0:T(8,128)(2,1)S(1)} %copy-done.1, s32[4,4]{1,0:T(4,128)S(1)} %copy-done.2, s32[32,4]{1,0:T(8,128)S(1)} %copy.5.vm_ref, bf16[4096,512]{1,0:T(8,128)(2,1)S(1)} %copy-done), custom_call_target="tpu_custom_call" | custom-call | flops 4294967296 | bytes 4194304 | tf_op jit(solution)/shard_map/pallas_call | solution.py:207
  142.4 0.8 copy.7
Async XLA Ops:
  0.8 2.2 %copy-start = (bf16[4096,512]{1,0:T(8,128)(2,1)S(1)}, bf16[4096,512]{1,0:T(8,128)(2,1)}, u32[]{:S(2)}) copy-start(bf16[4096,512]{1,0:T(8,128)(2,1)} %ints_ref.1) | copy-start | bytes 12582916
  3.0 1.0 copy-start.1
  4.0 0.7 copy-start.2

commit v2 on v1

v2 whole, which is shorter than its diff:
```python
import functools

import jax
import jax.numpy as jnp
from jax import lax
from jax.experimental import pallas as pl
from jax.experimental.pallas import tpu as pltpu
from jax.sharding import PartitionSpec as P

TILE = 128
NZ = 2
CORES = 2
MESH = pl.DeviceIdType.MESH


def kernel(sections, teams, columns, amps_ref, tm_ref, vm_ref, ints_ref, out_ref,
           mine, buf, v, texp, acc, part, got, load_sem, y_sem, send_sem, recv_sem, part_sem, got_sem):
    pieces, rows = mine.shape[0], texp.shape[0]
    panel = amps_ref.shape[1]
    row_tiles, tiles = rows // TILE, panel // TILE
    share = sections // teams
    levels = sections // (CORES * columns)
    step = CORES * columns
    width = min(share, step)
    depth, span = share // width, width // CORES
    s, t = lax.axis_index("section"), lax.axis_index("team")
    core, chip = lax.rem(s, CORES), lax.div(s, CORES)
    x, z = lax.rem(chip, columns), lax.div(chip, columns)
    group = lax.div(s, share)
    sibling = s + 1 - 2 * core
    first, offset = lax.div(t * share, step), lax.rem(t * share, step)

    def at(section, team):
        return {"section": section, "team": team}

    load = pltpu.make_async_copy(ints_ref, v, load_sem)
    load.start()

    barrier = pltpu.get_barrier_semaphore()

    def greet(section, team):
        pl.semaphore_signal(barrier, inc=1, device_id=at(section, team), device_id_type=MESH)

    greet(sibling, t)
    for d in range(1, columns):
        greet(s + CORES * (lax.rem(x + d, columns) - x), t)
    for d in range(1, teams):
        greet(s, lax.rem(t + d, teams))

    @pl.when(z > 0)
    def _():
        greet(s - step, t)

    @pl.when(z < levels - 1)
    def _():
        greet(s + step, t)

    partners = 1 + (columns - 1) + (teams - 1)
    partners = partners + jnp.where(z > 0, 1, 0) + jnp.where(z < levels - 1, 1, 0)

    def spread(table, i, c, j):
        row = table[i * tiles + c : i * tiles + c + 1, j * TILE : (j + 1) * TILE]
        return jnp.broadcast_to(row.astype(jnp.bfloat16), (TILE, TILE))

    shape = (mine.shape[1] - rows, NZ * TILE)
    table_row = lax.broadcasted_iota(jnp.int32, shape, 0)
    table_lane = lax.broadcasted_iota(jnp.int32, shape, 1)
    for h in range(pieces):
        hits = jnp.zeros(shape, jnp.float32)
        for i in range(row_tiles):
            before = jnp.int32(0)
            for c in range(tiles):
                one = tm_ref[h * row_tiles + i, c]
                for j in range(NZ):
                    hit = jnp.where(before == j, one, 0).astype(jnp.float32)
                    place = (table_row == i * tiles + c) & (table_lane >= j * TILE) & (table_lane < (j + 1) * TILE)
                    hits = jnp.where(place, hit, hits)
                before = before + one
        for i in range(row_tiles):
            r = (h * row_tiles + i) * TILE
            for j in range(NZ):
                total = None
                for c in range(tiles):
                    term = amps_ref[r : r + TILE, c * TILE : (c + 1) * TILE] * spread(hits, i, c, j)
                    total = term if total is None else total + term
                mine[h, i * TILE : (i + 1) * TILE, j * TILE : (j + 1) * TILE] = total
        mine[h, rows:, :] = hits.astype(jnp.bfloat16)

    def place_of(h, source, home):
        return (h * teams + source) * share + home

    def own(h):
        return place_of(h, t, lax.rem(s, share))

    @pl.when(group == t)
    def _():
        for h in range(pieces):
            buf[own(h)] = mine[h]

    pl.semaphore_wait(barrier, partners)

    def y_copy(h):
        return pltpu.make_async_remote_copy(
            src_ref=mine.at[h], dst_ref=buf.at[own(h)], send_sem=y_sem.at[h], recv_sem=recv_sem.at[own(h)],
            device_id=at(s, group), device_id_type=MESH)

    @pl.when(group != t)
    def _():
        for h in range(pieces):
            y_copy(h).start()

    phases = teams * pieces

    def slot(p, level, w):
        source = lax.rem(t + 1 + lax.div(p, pieces), teams)
        up, down = first + level, first + depth - 1 - level
        turn = first + lax.rem(z - first + level + depth, depth)
        row = jnp.where(z <= first, up, jnp.where(z >= first + depth - 1, down, turn))
        far = lax.rem(x + w, span)
        side = lax.rem(core + lax.div(w, span), CORES)
        home = row * step + offset + CORES * far + side
        u = home - t * share
        return source, u, place_of(lax.rem(p, pieces), source, u), home

    def relay(k, home, go):
        home_core, home_chip = lax.rem(home, CORES), lax.div(home, CORES)
        home_x, home_z = lax.rem(home_chip, columns), lax.div(home_chip, columns)
        straight = core == home_core
        column = straight & (x == home_x)

        def copy(kind, section):
            return pltpu.make_async_remote_copy(
                src_ref=buf.at[k], dst_ref=buf.at[k], send_sem=send_sem.at[kind, k], recv_sem=recv_sem.at[k],
                device_id=at(section, t), device_id_type=MESH)

        @pl.when(column & (z >= home_z) & (z < levels - 1))
        def _():
            go(copy(0, s + step))

        @pl.when(column & (z <= home_z) & (z > 0))
        def _():
            go(copy(1, s - step))

        for d in range(1, columns):
            @pl.when(column)
            def _():
                go(copy(2 + d, s + CORES * (lax.rem(x + d, columns) - x)))

        @pl.when(straight)
        def _():
            go(copy(2, sibling))

    def arrive(k, home, source):
        @pl.when((s != home) | (source != t))
        def _():
            pltpu.make_async_remote_copy(
                src_ref=buf.at[k], dst_ref=buf.at[k], send_sem=send_sem.at[2, k], recv_sem=recv_sem.at[k],
                device_id=at(sibling, t), device_id_type=MESH).wait_recv()

    def pass_on(p, level, w):
        source, _, k, home = slot(p, level, w)
        arrive(k, home, source)
        relay(k, home, lambda copy: copy.start())

    @pl.when(group == t)
    def _():
        for h in range(pieces):
            relay(own(h), s, lambda copy: copy.start())

    load.wait()

    @pl.loop(0, v.shape[0] // TILE)
    def _(k):
        here = pl.ds(pl.multiple_of(k * TILE, TILE), TILE)
        for c in range(v.shape[1] // TILE):
            lanes = slice(c * TILE, (c + 1) * TILE)
            v[here, lanes] = v[here, lanes] * jnp.full((TILE, TILE), vm_ref[k, c].astype(jnp.float32)).astype(jnp.bfloat16)

    def part_copy(p):
        d, h = p // pieces + 1, p % pieces
        there = (teams - d - 1) * pieces + h
        return pltpu.make_async_remote_copy(
            src_ref=part.at[p], dst_ref=got.at[there], send_sem=part_sem.at[p],
            recv_sem=got_sem.at[there], device_id=at(s, lax.rem(t + d, teams)), device_id_type=MESH)

    def columns_of(p):
        for level in range(1 if p >= phases - pieces else 0, depth):
            pass_on(p, level, 0)

    def rest_of(p):
        for level in range(depth):
            for w in range(1, span):
                pass_on(p, level, w)

    def compute(p):
        acc[...] = jnp.zeros_like(acc)

        @pl.loop(0, share)
        def _(n):
            level, w = lax.div(n, width), lax.rem(n, width)
            source, u, k, home = slot(p, level, w)

            @pl.when(w >= span)
            def _():
                arrive(k, home, source)

            table = buf[k, rows:, :].astype(jnp.float32)
            for i in range(row_tiles):
                for c in range(tiles):
                    tile = None
                    for j in range(NZ):
                        term = buf[k, i * TILE : (i + 1) * TILE, j * TILE : (j + 1) * TILE] * spread(table, i, c, j)
                        tile = term if tile is None else tile + term
                    texp[i * TILE : (i + 1) * TILE, c * TILE : (c + 1) * TILE] = tile
            here = pl.ds(pl.multiple_of(u * panel, panel), panel)
            acc[...] += jnp.dot(texp[...], v[here, :], preferred_element_type=jnp.float32)

    for p in range(phases - pieces, phases):
        source, _, k, home = slot(p, 0, 0)

        @pl.when(s != home)
        def _():
            pass_on(p, 0, 0)

    columns_of(0)
    for p in range(phases):
        if p + 1 < phases:
            columns_of(p + 1)
        rest_of(p)
        compute(p)
        if p < phases - pieces:
            part[p] = acc[...]
            part_copy(p).start()
        else:
            h = p - (phases - pieces)
            for d in range(1, teams):
                there = (d - 1) * pieces + h
                part_copy((teams - d - 1) * pieces + h).wait_recv()
                acc[...] += got[there]
            out_ref[h * rows : (h + 1) * rows, :] = acc[...].astype(out_ref.dtype)

    @pl.when(group != t)
    def _():
        for h in range(pieces):
            y_copy(h).wait_send()

    @pl.loop(0, phases * share)
    def _(n):
        p, n = lax.div(n, share), lax.rem(n, share)
        _, _, k, home = slot(p, lax.div(n, width), lax.rem(n, width))
        relay(k, home, lambda copy: copy.wait_send())

    for p in range(phases - pieces):
        part_copy(p).wait_send()


def shards(sections, teams, columns, amps, t_mask, ints, v_mask):
    rows, panel = amps.shape
    depth, ab_cols = ints.shape
    row_tiles = rows // TILE
    pieces = 2 if row_tiles % 2 == 0 else 1
    piece = rows // pieces
    table = t_mask.shape[0] * t_mask.shape[1] // pieces
    message = (piece + -(-table // 16) * 16, NZ * TILE)
    slots, parts = pieces * sections, pieces * (teams - 1)
    smem = pl.BlockSpec(memory_space=pltpu.SMEM)
    vmem = pl.BlockSpec(memory_space=pltpu.VMEM)
    return pl.pallas_call(
        functools.partial(kernel, sections, teams, columns),
        out_shape=jax.ShapeDtypeStruct((rows, ab_cols), jnp.bfloat16),
        in_specs=[vmem, smem, smem, pl.BlockSpec(memory_space=pl.ANY)],
        out_specs=vmem,
        scratch_shapes=[
            pltpu.VMEM((pieces, *message), jnp.bfloat16),
            pltpu.VMEM((slots, *message), jnp.bfloat16),
            pltpu.VMEM((depth, ab_cols), jnp.bfloat16),
            pltpu.VMEM((piece, panel), jnp.bfloat16),
            pltpu.VMEM((piece, ab_cols), jnp.float32),
            pltpu.VMEM((parts, piece, ab_cols), jnp.float32),
            pltpu.VMEM((parts, piece, ab_cols), jnp.float32),
            pltpu.SemaphoreType.DMA,
            pltpu.SemaphoreType.DMA((pieces,)),
            pltpu.SemaphoreType.DMA((2 + columns, slots)),
            pltpu.SemaphoreType.DMA((slots,)),
            pltpu.SemaphoreType.DMA((parts,)),
            pltpu.SemaphoreType.DMA((parts,)),
        ],
        compiler_params=pltpu.CompilerParams(
            collective_id=0, has_side_effects=True, vmem_limit_bytes=48 * 2**20
        ),
        cost_estimate=pl.CostEstimate(
            flops=2 * teams * rows * depth * ab_cols, bytes_accessed=2 * depth * ab_cols, transcendentals=0
        ),
    )(amps, t_mask, v_mask, ints)


def solution(mesh):
    sections, teams = mesh.shape["section"], mesh.shape["team"]
    chips = sections // CORES
    columns = 1
    while (2 * columns) ** 2 <= chips and chips % (2 * columns) == 0:
        columns *= 2
    spec = P("team", "section")
    return jax.shard_map(
        functools.partial(shards, sections, teams, columns),
        mesh=mesh, in_specs=(spec,) * 4, out_specs=spec, check_vma=False)
```

time: 143 us -> 67.3 us (0.47)
  the two profiles are of different devices: /device:TPU:4 before, /device:TPU:0 now
where the time goes in v2:
time: 67.3 us; the launch traced here: 67.1 us
  Pallas kernels  61.6 us (92%)
  local copies, waits for them, and re-layouts  5.47 us (8%)
    pallas_call x1, Pallas kernels, shards(): pl.pallas_call(functools.partial(kernel, sections, teams, columns), out_s...  61.6 us
    unnamed x8, local copies, waits for them, and re-layouts  5.47 us

profile of v2, /device:TPU:0, one launch (start us, length us, event | category | flops | bytes accessed | tf_op | source)
XLA Modules:
  0.0 67.1 jit_solution(14724780368214341871)
XLA Ops:
  0.0 0.8 %copy.5.vm_ref = s32[32,4]{1,0:T(8,128)S(1)} copy(s32[32,4]{0,1:T(4,128)} %param.7) | data formatting | bytes 1024 | tf_op args[3]
  0.8 0.0 copy-start
  0.8 2.2 %copy-done = bf16[4096,512]{1,0:T(8,128)(2,1)S(1)} copy-done((bf16[4096,512]{1,0:T(8,128)(2,1)S(1)}, bf16[4096,512]{1,0:T(8,128)(2,1)}, u32[]{:S(2)}) %copy-start) | copy-done | bytes 4194328
  3.0 0.0 copy-start.1
  3.0 1.0 %copy-done.1 = bf16[512,512]{1,0:T(8,128)(2,1)S(1)} copy-done((bf16[512,512]{1,0:T(8,128)(2,1)S(1)}, bf16[512,512]{1,0:T(8,128)(2,1)}, u32[]{:S(2)}) %copy-start.1) | copy-done | bytes 524312
  4.0 0.0 copy-start.2
  4.0 0.7 %copy-done.2 = s32[4,4]{1,0:T(4,128)S(1)} copy-done((s32[4,4]{1,0:T(4,128)S(1)}, s32[4,4]{1,0:T(4,128)}, u32[]{:S(2)}) %copy-start.2) | copy-done | bytes 88
  4.7 61.6 %shard_map.46 = bf16[512,512]{1,0:T(8,128)(2,1)S(1)} custom-call(bf16[512,512]{1,0:T(8,128)(2,1)S(1)} %copy-done.1, s32[4,4]{1,0:T(4,128)S(1)} %copy-done.2, s32[32,4]{1,0:T(8,128)S(1)} %copy.5.vm_ref, bf16[4096,512]{1,0:T(8,128)(2,1)S(1)} %copy-done), custom_call_target="tpu_custom_call" | custom-call | flops 4294967296 | bytes 4194304 | tf_op jit(solution)/shard_map/pallas_call | solution.py:268
  66.3 0.8 %copy.7 = bf16[512,512]{1,0:T(8,128)(2,1)} copy(bf16[512,512]{1,0:T(8,128)(2,1)S(1)} %shard_map.46) | data formatting | bytes 1048576
Async XLA Ops:
  0.8 2.2 %copy-start = (bf16[4096,512]{1,0:T(8,128)(2,1)S(1)}, bf16[4096,512]{1,0:T(8,128)(2,1)}, u32[]{:S(2)}) copy-start(bf16[4096,512]{1,0:T(8,128)(2,1)} %ints_ref.1) | copy-start | bytes 12582916
  3.0 1.0 %copy-start.1 = (bf16[512,512]{1,0:T(8,128)(2,1)S(1)}, bf16[512,512]{1,0:T(8,128)(2,1)}, u32[]{:S(2)}) copy-start(bf16[512,512]{1,0:T(8,128)(2,1)} %amps_ref.1) | copy-start | bytes 1572868
  4.0 0.7 %copy-start.2 = (s32[4,4]{1,0:T(4,128)S(1)}, s32[4,4]{1,0:T(4,128)}, u32[]{:S(2)}) copy-start(s32[4,4]{1,0:T(4,128)} %tm_ref.1) | copy-start | bytes 196

commit v3 on v2

--- a/solution.py
+++ b/solution.py
@@ -167,15 +167,6 @@
         for h in range(pieces):
             relay(own(h), s, lambda copy: copy.start())
 
-    load.wait()
-
-    @pl.loop(0, v.shape[0] // TILE)
-    def _(k):
-        here = pl.ds(pl.multiple_of(k * TILE, TILE), TILE)
-        for c in range(v.shape[1] // TILE):
-            lanes = slice(c * TILE, (c + 1) * TILE)
-            v[here, lanes] = v[here, lanes] * jnp.full((TILE, TILE), vm_ref[k, c].astype(jnp.float32)).astype(jnp.bfloat16)
-
     def part_copy(p):
         d, h = p // pieces + 1, p % pieces
         there = (teams - d - 1) * pieces + h
@@ -223,6 +214,15 @@
             pass_on(p, 0, 0)
 
     columns_of(0)
+    load.wait()
+
+    @pl.loop(0, v.shape[0] // TILE)
+    def _(k):
+        here = pl.ds(pl.multiple_of(k * TILE, TILE), TILE)
+        for c in range(v.shape[1] // TILE):
+            lanes = slice(c * TILE, (c + 1) * TILE)
+            v[here, lanes] = v[here, lanes] * jnp.full((TILE, TILE), vm_ref[k, c].astype(jnp.float32)).astype(jnp.bfloat16)
+
     for p in range(phases):
         if p + 1 < phases:
             columns_of(p + 1)
@@ -286,7 +286,7 @@
             pltpu.SemaphoreType.DMA((parts,)),
         ],
         compiler_params=pltpu.CompilerParams(
-            collective_id=0, has_side_effects=True, vmem_limit_bytes=48 * 2**20
+            collective_id=0, has_side_effects=True, vmem_limit_bytes=60 * 2**20
         ),
         cost_estimate=pl.CostEstimate(
             flops=2 * teams * rows * depth * ab_cols, bytes_accessed=2 * depth * ab_cols, transcendentals=0

time: 67.3 us -> 65.9 us (0.979)
  local copies, waits for them, and re-layouts: 5.47 us -> 3.23 us
  Pallas kernels: 61.6 us -> 62.4 us
    unnamed x8 -> x2, local copies, waits for them, and re-layouts: 5.47 us -> 3.23 us
    pallas_call x1, Pallas kernels: 61.6 us -> 62.4 us  [shards(): pl.pallas_call(functools.partial(kernel, sections, teams, columns), out_s...]
where the time goes in v3:
time: 65.9 us; the launch traced here: 65.6 us
  Pallas kernels  62.4 us (95%)
  local copies, waits for them, and re-layouts  3.23 us (5%)
    pallas_call x1, Pallas kernels, shards(): pl.pallas_call(functools.partial(kernel, sections, teams, columns), out_s...  62.4 us
    unnamed x2, local copies, waits for them, and re-layouts  3.23 us

profile of v3, /device:TPU:0, one launch (start us, length us, event | category | flops | bytes accessed | tf_op | source)
XLA Modules:
  0.0 65.6 jit_solution(1664523461337345417)
XLA Ops:
  0.0 1.4 %copy.5.vm_ref = s32[32,4]{1,0:T(8,128)} copy(s32[32,4]{0,1:T(4,128)} %param.7) | data formatting | bytes 1024 | tf_op args[3]
  1.4 62.4 %shard_map.46 = bf16[512,512]{1,0:T(8,128)(2,1)} custom-call(bf16[512,512]{1,0:T(8,128)(2,1)} %amps_ref.1, s32[4,4]{1,0:T(4,128)} %tm_ref.1, s32[32,4]{1,0:T(8,128)} %copy.5.vm_ref, bf16[4096,512]{1,0:T(8,128)(2,1)} %ints_ref.1), custom_call_target="tpu_custom_call" | custom-call | flops 4294967296 | bytes 4194304 | tf_op jit(solution)/shard_map/pallas_call | solution.py:268
  63.7 1.9 %copy.7 = bf16[512,512]{1,0:T(8,128)(2,1)} copy(bf16[512,512]{1,0:T(8,128)(2,1)} %shard_map.46) | data formatting | bytes 1048576

commit v4 on v3

--- a/solution.py
+++ b/solution.py
@@ -224,9 +224,9 @@
             v[here, lanes] = v[here, lanes] * jnp.full((TILE, TILE), vm_ref[k, c].astype(jnp.float32)).astype(jnp.bfloat16)
 
     for p in range(phases):
+        rest_of(p)
         if p + 1 < phases:
             columns_of(p + 1)
-        rest_of(p)
         compute(p)
         if p < phases - pieces:
             part[p] = acc[...]

time: 65.9 us -> 65.1 us (0.988)
  Pallas kernels: 62.4 us -> 61.6 us
    pallas_call x1, Pallas kernels: 62.4 us -> 61.6 us  [shards(): pl.pallas_call(functools.partial(kernel, sections, teams, columns), out_s...]
where the time goes in v4:
time: 65.1 us; the launch traced here: 64.8 us
  Pallas kernels  61.6 us (95%)
  local copies, waits for them, and re-layouts  3.23 us (5%)
    pallas_call x1, Pallas kernels, shards(): pl.pallas_call(functools.partial(kernel, sections, teams, columns), out_s...  61.6 us
    unnamed x2, local copies, waits for them, and re-layouts  3.23 us

profile of v4, /device:TPU:0, one launch (start us, length us, event | category | flops | bytes accessed | tf_op | source)
XLA Modules:
  0.0 64.8 jit_solution(14192756898211734587)
XLA Ops:
  0.0 1.4 %copy.5.vm_ref = s32[32,4]{1,0:T(8,128)} copy(s32[32,4]{0,1:T(4,128)} %param.7) | data formatting | bytes 1024 | tf_op args[3]
  1.4 61.6 %shard_map.46 = bf16[512,512]{1,0:T(8,128)(2,1)} custom-call(bf16[512,512]{1,0:T(8,128)(2,1)} %amps_ref.1, s32[4,4]{1,0:T(4,128)} %tm_ref.1, s32[32,4]{1,0:T(8,128)} %copy.5.vm_ref, bf16[4096,512]{1,0:T(8,128)(2,1)} %ints_ref.1), custom_call_target="tpu_custom_call" | custom-call | flops 4294967296 | bytes 4194304 | tf_op jit(solution)/shard_map/pallas_call | solution.py:268
  63.0 1.9 %copy.7 = bf16[512,512]{1,0:T(8,128)(2,1)} copy(bf16[512,512]{1,0:T(8,128)(2,1)} %shard_map.46) | data formatting | bytes 1048576
